TPU v7x, 256 devices: a whole 4x4x8 slice. The times are simulated.
256 devices in a mesh: kp: 64 (over z, y, core), eig: 4 (over x).
Axes of the slice: x: 4, y: 4, z: 8, core: 2. Of those that a mesh axis runs over, the one named last changes fastest.
Arguments:
- cond_dens: bfloat16 [64, 64, 64, 2048], P(None, 'kp', None, 'eig'), may hold values from -0.75 to 0.75
- val_dens: bfloat16 [64, 64, 64, 2048], P('kp', None, None, 'eig'), may hold values from -0.75 to 0.75
- trial_vecs: bfloat16 [32, 64, 512], replicated, may hold values from -6 to 6
- eig_vals: float32 [2048], P('eig'), may hold values from 0.005 to 0.05
- block_pairs: int32 [64, 2], replicated, may hold values from 0 to 31, as said below
- slot_block: int32 [64], replicated, may hold values from 0 to 63, each once
Outputs:
- kernel_image: float32 [2048, 512], P('kp', 'eig')
Inputs may be any that keep to these rules, and one draw needn't show every extreme that they name: `block_pairs`: distinct pairs with k <= k2.
All inputs are finite; a program needn't handle non-finite values.
Results may differ from a plain program's by a relative error of at most 0.0065.
Values may be sent and summed in bfloat16 or wider, within the bound.
No kernel may reach another device: no remote copies, remote signals or barrier semaphores. Data moves between devices by JAX's collectives and lax.ppermute only.
A program may use at most 128 MiB of HBM per device.

v0:
```python
import functools
import jax
import jax.numpy as jnp
from jax import lax
from jax.experimental import pallas as pl
from jax.experimental.pallas import tpu as pltpu
from jax.sharding import Mesh, PartitionSpec as P

F32 = jnp.float32
BF16 = jnp.bfloat16
MIB = 1024 * 1024


def gather_kernel(first, width, chunks, order_ref, cond_ref, out_ref, held, in_sems, out_sems):
    size = held.shape[0] // chunks

    for chunk in range(chunks):
        @pl.loop(chunk * size, (chunk + 1) * size, unroll=8)
        def _(slot):
            pltpu.make_async_copy(
                cond_ref.at[order_ref[slot], :, :, pl.ds(first, width)],
                held.at[slot],
                in_sems.at[chunk],
            ).start()

    stores = []
    for chunk in range(chunks):
        part = pl.ds(chunk * size, size)
        pltpu.make_async_copy(held.at[part], held.at[part], in_sems.at[chunk]).wait()
        stores.append(pltpu.make_async_copy(held.at[part], out_ref.at[part], out_sems.at[chunk]))
        stores[-1].start()
    for store in stores:
        store.wait()


def gather_rows(cond, order, first, width, chunks):
    count, one, depth, _ = cond.shape
    shape = (count, one, depth, width)
    return pl.pallas_call(
        functools.partial(gather_kernel, first, width, chunks),
        out_shape=jax.ShapeDtypeStruct(shape, cond.dtype),
        in_specs=[pl.BlockSpec(memory_space=pltpu.SMEM), pl.BlockSpec(memory_space=pl.ANY)],
        out_specs=pl.BlockSpec(memory_space=pl.ANY),
        scratch_shapes=[
            pltpu.VMEM(shape, cond.dtype),
            pltpu.SemaphoreType.DMA((chunks,)),
            pltpu.SemaphoreType.DMA((chunks,)),
        ],
        compiler_params=pltpu.CompilerParams(vmem_limit_bytes=60 * MIB),
        cost_estimate=pl.CostEstimate(
            flops=0, bytes_accessed=4 * count * depth * width, transcendentals=0
        ),
        name="gather_rows",
    )(order, cond)


def expand_kernel(nvec, x_ref, v_ref, eig_ref, *out_refs):
    groups = x_ref.shape[0] // nvec
    x = x_ref[...]
    scale = eig_ref[...]
    for pair in range(v_ref.shape[0] // 2):
        low = jnp.dot(x, v_ref[2 * pair], preferred_element_type=F32) * scale
        high = jnp.dot(x, v_ref[2 * pair + 1], preferred_element_type=F32) * scale
        rows = pl.ds(pair * 2 * nvec, 2 * nvec)
        for b in range(groups):
            both = jnp.concatenate(
                [low[b * nvec : (b + 1) * nvec], high[b * nvec : (b + 1) * nvec]], axis=0
            ).astype(BF16)
            start = 0
            for out_ref in out_refs:
                width = out_ref.shape[1] // groups
                out_ref[rows, pl.ds(b * width, width)] = both[:, start : start + width]
                start += width


def expand(x, v, eig, widths, nvec, step):
    count, depth, lanes = v.shape
    rows = x.shape[0]
    groups = rows // nvec
    return pl.pallas_call(
        functools.partial(expand_kernel, nvec),
        out_shape=[
            jax.ShapeDtypeStruct((count * nvec, groups * width), BF16) for width in widths
        ],
        grid=(count // step,),
        in_specs=[
            pl.BlockSpec((rows, depth), lambda i: (0, 0)),
            pl.BlockSpec((step, depth, lanes), lambda i: (i, 0, 0)),
            pl.BlockSpec((1, lanes), lambda i: (0, 0)),
        ],
        out_specs=[
            pl.BlockSpec((step * nvec, groups * width), lambda i: (i, 0)) for width in widths
        ],
        compiler_params=pltpu.CompilerParams(vmem_limit_bytes=60 * MIB),
        cost_estimate=pl.CostEstimate(
            flops=2 * rows * depth * lanes * count,
            bytes_accessed=2 * count * rows * lanes + 2 * count * depth * lanes,
            transcendentals=0,
        ),
        name="expand",
    )(x, v, eig)


def product(c, u):
    return lax.dot_general(c, u, (((1,), (1,)), ((), ())), preferred_element_type=F32)


def first_kernel(u2_ref, ct_ref, u1_ref, c_ref, fwd_ref, mir_ref):
    @pl.when(pl.program_id(0) == 0)
    def _():
        fwd_ref[...] = jnp.zeros_like(fwd_ref)
        mir_ref[...] = jnp.zeros_like(mir_ref)

    for u_ref, rows_ref, sum_ref in ((u2_ref, ct_ref, fwd_ref), (u1_ref, c_ref, mir_ref)):
        rows = jnp.concatenate([rows_ref[j] for j in range(rows_ref.shape[0])], axis=1)
        sum_ref[...] += product(rows, u_ref[...])


def contract_first(u2, ct, u1, c, step):
    rows = u2.shape[0]
    groups, cols, width = c.shape
    u_spec = pl.BlockSpec((rows, step * width), lambda i: (0, i))
    c_spec = pl.BlockSpec((step, cols, width), lambda i: (i, 0, 0))
    sum_spec = pl.BlockSpec((cols, rows), lambda i: (0, 0))
    sums = jax.ShapeDtypeStruct((cols, rows), F32)
    return pl.pallas_call(
        first_kernel,
        out_shape=[sums, sums],
        grid=(groups // step,),
        in_specs=[u_spec, c_spec, u_spec, c_spec],
        out_specs=[sum_spec, sum_spec],
        compiler_params=pltpu.CompilerParams(vmem_limit_bytes=60 * MIB),
        cost_estimate=pl.CostEstimate(
            flops=4 * rows * cols * groups * width,
            bytes_accessed=4 * groups * width * (rows + cols),
            transcendentals=0,
        ),
        name="contract_first",
    )(u2, ct, u1, c)


def last_kernel(
    step, ahead, pad, u2_ref, u1_ref, c_hbm, fwd_ref, mir_ref, out_ref, c_ref, u_ref, flip, c_sem, u_sems
):
    groups, cols, width = c_ref.shape
    blocks = groups // step
    lanes = step * width
    fetch_c = pltpu.make_async_copy(c_hbm, c_ref, c_sem)
    fetches = [
        pltpu.make_async_copy(
            source.at[:, pl.ds(block * lanes, lanes)],
            u_ref.at[which * blocks + block],
            u_sems.at[which * blocks + block],
        )
        for which, source in ((0, u1_ref), (1, u2_ref))
        for block in range(blocks)
    ]
    fetch_c.start()
    for index in range(ahead):
        fetches[index].start()

    def arrived(index):
        fetches[index].wait()
        if index + ahead < len(fetches):
            fetches[index + ahead].start()
        return u_ref[index]

    fetch_c.wait()
    for c in range(groups):
        flip[pl.ds(c * pad, cols)] = c_ref[c].astype(F32)
    forward, mirror = fwd_ref[...], mir_ref[...]
    for block in range(blocks):
        rows = jnp.concatenate([c_ref[block * step + j] for j in range(step)], axis=1)
        mirror = mirror + product(rows, arrived(block))
    for block in range(blocks):
        rows = jnp.concatenate(
            [
                flip[pl.ds(block * step + j, groups, stride=pad)].astype(BF16)
                for j in range(step)
            ],
            axis=1,
        )
        forward = forward + product(rows, arrived(blocks + block))
    pieces, _, part, half_lanes = out_ref.shape
    parts = cols // part
    for which, total in ((0, forward), (1, mirror)):
        total = total.astype(BF16)
        for piece in range(pieces):
            half, eig = piece // parts, piece % parts
            out_ref[piece, which] = total[
                eig * part : (eig + 1) * part, half * half_lanes : (half + 1) * half_lanes
            ]


def contract_last(u2, u1, c, forward, mirror, pieces, step, ahead):
    rows = u2.shape[0]
    groups, cols, width = c.shape
    pad = cols + 8
    copies = 2 * groups // step
    whole = pl.BlockSpec(memory_space=pltpu.VMEM)
    away = pl.BlockSpec(memory_space=pl.ANY)
    return pl.pallas_call(
        functools.partial(last_kernel, step, ahead, pad),
        out_shape=jax.ShapeDtypeStruct(pieces, BF16),
        in_specs=[away, away, away, whole, whole],
        out_specs=whole,
        scratch_shapes=[
            pltpu.VMEM((groups, cols, width), BF16),
            pltpu.VMEM((copies, rows, step * width), BF16),
            pltpu.VMEM((groups * pad, width), F32),
            pltpu.SemaphoreType.DMA,
            pltpu.SemaphoreType.DMA((copies,)),
        ],
        compiler_params=pltpu.CompilerParams(vmem_limit_bytes=60 * MIB),
        cost_estimate=pl.CostEstimate(
            flops=4 * rows * cols * groups * width,
            bytes_accessed=4 * groups * width * (rows + cols),
            transcendentals=0,
        ),
        name="contract_last",
    )(u2, u1, c, forward, mirror)


def per_device(cond_dens, val_dens, trial_vecs, eig_vals, block_pairs, slot_block):
    kpoints, nv_bands, columns = trial_vecs.shape
    nc_bands = cond_dens.shape[2]
    nvec = columns // nc_bands
    lanes = cond_dens.shape[3]
    cores, eigs = lax.axis_size("c"), lax.axis_size("x")
    chip = lax.axis_index("z") * lax.axis_size("y") + lax.axis_index("y")
    slot = chip * cores + lax.axis_index("c")
    kp = ("z", "y", "c")

    late = 128
    early = lanes - late
    sent_early = gather_rows(cond_dens, slot_block, 0, early, 4)
    owned_early = lax.all_to_all(sent_early, kp, split_axis=0, concat_axis=0, tiled=True)
    pair = block_pairs[slot_block[slot]]
    near = trial_vecs[pair[0]] * (pair[0] < pair[1]).astype(BF16)
    far = trial_vecs[pair[1]]
    near = near.reshape(nv_bands, columns).T
    far = far.reshape(nv_bands, columns).T
    eig = eig_vals[None, :]
    values = val_dens[0]
    u2_early, u2_late = expand(far, values, eig, (early, late), nvec, 4)
    u1_early, u1_late = expand(near, values.transpose(1, 0, 2), eig, (early, late), nvec, 4)

    sent_late = gather_rows(cond_dens, slot_block, early, late, 2)
    both = block_pairs[lax.dynamic_slice_in_dim(slot_block, chip * cores, cores)]
    hits = (jnp.arange(kpoints, dtype=jnp.int32) == both[:, :, None]).astype(F32)
    sent_late, owned_early, u2_early, u1_early, hits = lax.optimization_barrier(
        (sent_late, owned_early, u2_early, u1_early, hits)
    )
    owned_late = lax.all_to_all(sent_late, kp, split_axis=0, concat_axis=0, tiled=True)
    owned_early = owned_early.reshape(nc_bands, nc_bands, early)
    owned_late = owned_late.reshape(nc_bands, nc_bands, late)

    forward, mirror = contract_first(
        u2_early, owned_early.transpose(1, 0, 2), u1_early, owned_early, 8
    )
    part_rows = nc_bands // eigs
    half_lanes = nv_bands * nvec // cores
    pieces = (cores * eigs, 2, part_rows, half_lanes)
    sums = contract_last(u2_late, u1_late, owned_late, forward, mirror, pieces, 8, 4)

    arrived = lax.all_to_all(sums, ("c", "x"), split_axis=0, concat_axis=0, tiled=True)
    arrived = arrived.reshape(cores, eigs, 2, part_rows, half_lanes).astype(F32).sum(1)
    placed = jnp.zeros((kpoints, part_rows, half_lanes), F32)
    for core in range(cores):
        for which in range(2):
            placed = placed + hits[core, which][:, None, None] * arrived[core, which]
    image = lax.all_to_all(placed.astype(BF16), ("z", "y"), split_axis=0, concat_axis=0, tiled=True)
    image = image.astype(F32).sum(0).reshape(part_rows, nv_bands // cores, nvec)
    return image.transpose(1, 0, 2).reshape(nv_bands // cores, part_rows * nvec)


def solution(mesh):
    kp, eig = mesh.devices.shape
    fine = Mesh(mesh.devices.reshape(8, kp // 16, 2, eig), ("z", "y", "c", "x"))
    kp_axes = ("z", "y", "c")
    return jax.shard_map(
        per_device,
        mesh=fine,
        in_specs=(
            P(None, kp_axes, None, "x"),
            P(kp_axes, None, None, "x"),
            P(),
            P("x"),
            P(),
            P(),
        ),
        out_specs=P(kp_axes, "x"),
        check_vma=False,
    )
```

profile of v0, /device:TPU:2, one launch (start us, length us, event | category | flops | bytes accessed | tf_op | source)
XLA Modules:
  0.0 165.1 jit_solution(10233744739658591704)
XLA Ops:
  0.0 3.5 %gather_rows.3 = bf16[64,1,64,384]{3,2,1,0:T(8,128)(2,1)} custom-call(s32[64]{0:T(128)} %order_ref.3, bf16[64,1,64,512]{3,2,1,0:T(8,128)(2,1)} %cond_ref.3), custom_call_target="tpu_custom_call" | custom-call | bytes 6291456 | tf_op jit(solution)/shard_map/gather_rows/pallas_call | solution.py:39
  3.6 12.1 %all-to-all-start = ((bf16[64,1,64,384]{3,2,1,0:T(8,128)(2,1)}), bf16[64,1,64,384]{3,2,1,0:T(8,128)(2,1)S(1)}, u32[]{:S(2)}, u32[]{:S(2)}) async-start(bf16[64,1,64,384]{3,2,1,0:T(8,128)(2,1)} %gather_rows.3), calls=%async_computation | async-start | bytes 6291456 | tf_op jit(solution)/shard_map/all_to_all | solution.py:237
  15.7 0.6 dynamic_slice.15
  18.3 0.5 fusion
  22.8 2.7 %gather_rows.2 = bf16[64,1,64,128]{3,2,1,0:T(8,128)(2,1)} custom-call(s32[64]{0:T(128)} %order_ref.3, bf16[64,1,64,512]{3,2,1,0:T(8,128)(2,1)} %cond_ref.3), custom_call_target="tpu_custom_call" | custom-call | bytes 2097152 | tf_op jit(solution)/shard_map/gather_rows/pallas_call | solution.py:39
  26.8 0.9 constant_dynamic-slice_fusion
  27.7 0.1 copy.43
  27.8 0.8 copy.33
  28.6 6.5 %copy.45 = bf16[1,64,64,512]{3,1,2,0:T(8,128)(2,1)} copy(bf16[1,64,64,512]{3,2,1,0:T(8,128)(2,1)} %param.7) | data formatting | bytes 8388608 | tf_op args[1]
  35.2 0.6 gather_fusion
  35.7 0.7 multiply_bitcast_fusion.x_ref
  36.4 18.9 %expand.3 = (bf16[512,24576]{1,0:T(8,128)(2,1)}, bf16[512,8192]{1,0:T(8,128)(2,1)}) custom-call(bf16[512,64]{1,0:T(8,128)(2,1)} %multiply_bitcast_fusion.x_ref, bf16[64,64,512]{2,1,0:T(8,128)(2,1)} %bitcast.47, f32[1,512]{1,0:T(1,128)} %bitcast.51), custom_call_target="tpu_custom_call" | custom-call | flops 2147483648 | bytes 37748736 | tf_op jit(solution)/shard_map/expand/pallas_call | solution.py:80
  55.3 18.9 %expand.2 = (bf16[512,24576]{1,0:T(8,128)(2,1)}, bf16[512,8192]{1,0:T(8,128)(2,1)}) custom-call(bf16[512,64]{1,0:T(8,128)(2,1)} %bitcast.50, bf16[64,64,512]{2,1,0:T(8,128)(2,1)} %bitcast.46, f32[1,512]{1,0:T(1,128)} %bitcast.52), custom_call_target="tpu_custom_call" | custom-call | flops 2147483648 | bytes 37748736 | tf_op jit(solution)/shard_map/expand/pallas_call | solution.py:80
  74.3 15.3 %all-to-all-done = bf16[64,1,64,384]{3,2,1,0:T(8,128)(2,1)S(1)} async-done(((bf16[64,1,64,384]{3,2,1,0:T(8,128)(2,1)}), bf16[64,1,64,384]{3,2,1,0:T(8,128)(2,1)S(1)}, u32[]{:S(2)}, u32[]{:S(2)}) %all-to-all-start) | async-done | bytes 3145760 | tf_op jit(solution)/shard_map/all_to_all | solution.py:237
  89.6 5.7 %all-to-all-start.1 = ((bf16[64,1,64,128]{3,2,1,0:T(8,128)(2,1)}), bf16[64,1,64,128]{3,2,1,0:T(8,128)(2,1)}, u32[]{:S(2)}, u32[]{:S(2)}) async-start(bf16[64,1,64,128]{3,2,1,0:T(8,128)(2,1)} %gather_rows.2), calls=%async_computation.1 | async-start | bytes 2097152 | tf_op jit(solution)/shard_map/all_to_all | solution.py:254
  95.3 3.6 %copy.38.ct_ref = bf16[64,64,384]{2,1,0:T(8,128)(2,1)} copy(bf16[64,64,384]{2,0,1:T(8,128)(2,1)S(1)} %bitcast.44) | data formatting | bytes 6291456 | tf_op jit(solution)/shard_map/transpose | solution.py:259
  98.9 23.2 %contract_first.1 = (f32[64,512]{1,0:T(8,128)}, f32[64,512]{1,0:T(8,128)}) custom-call(bf16[512,24576]{1,0:T(8,128)(2,1)} %get-tuple-element.22.u2_ref, bf16[64,64,384]{2,1,0:T(8,128)(2,1)} %copy.38.ct_ref, bf16[512,24576]{1,0:T(8,128)(2,1)} %get-tuple-element.24.u1_ref, bf16[64,64,384]{2,1,0:T(8,128)(2,1)} %bitcast.45), custom_call_target="tpu_custom_call" | custom-call | flops 3221225472 | bytes 56623104 | tf_op jit(solution)/shard_map/contract_first/pallas_call | solution.py:126
  122.1 1.8 %all-to-all-done.1 = bf16[64,1,64,128]{3,2,1,0:T(8,128)(2,1)} async-done(((bf16[64,1,64,128]{3,2,1,0:T(8,128)(2,1)}), bf16[64,1,64,128]{3,2,1,0:T(8,128)(2,1)}, u32[]{:S(2)}, u32[]{:S(2)}) %all-to-all-start.1) | async-done | bytes 1048608 | tf_op jit(solution)/shard_map/all_to_all | solution.py:254
  123.9 10.1 %contract_last.1 = bf16[8,2,16,256]{3,2,1,0:T(8,128)(2,1)} custom-call(bf16[512,8192]{1,0:T(8,128)(2,1)} %get-tuple-element.19.u2_ref, bf16[512,8192]{1,0:T(8,128)(2,1)} %get-tuple-element.20.u1_ref, bf16[64,64,128]{2,1,0:T(8,128)(2,1)} %bitcast.12.c_hbm, f32[64,512]{1,0:T(8,128)} %get-tuple-element.25.fwd_ref, f32[64,512]{1,0:T(8,128)} %get-tuple-element.26.mir_ref), custom_call_target="tpu_custom_call" | custom-call | flops 1073741824 | bytes 18874368 | tf_op jit(solution)/shard_map/contract_last/pallas_call | solution.py:202
  133.9 4.8 %all-to-all-start.2 = ((bf16[8,2,16,256]{3,2,1,0:T(8,128)(2,1)}), bf16[8,2,16,256]{3,2,1,0:T(8,128)(2,1)S(1)}, u32[]{:S(2)}, u32[]{:S(2)}) async-start(bf16[8,2,16,256]{3,2,1,0:T(8,128)(2,1)} %contract_last.1), calls=%async_computation.2 | async-start | bytes 262144 | tf_op jit(solution)/shard_map/all_to_all | solution.py:266
  138.8 4.5 %all-to-all-done.2 = bf16[8,2,16,256]{3,2,1,0:T(8,128)(2,1)S(1)} async-done(((bf16[8,2,16,256]{3,2,1,0:T(8,128)(2,1)}), bf16[8,2,16,256]{3,2,1,0:T(8,128)(2,1)S(1)}, u32[]{:S(2)}, u32[]{:S(2)}) %all-to-all-start.2) | async-done | bytes 131104 | tf_op jit(solution)/shard_map/all_to_all | solution.py:266
  143.3 0.2 add_convert_fusion
  143.5 20.7 %all_to_all.20 = bf16[32,16,256]{2,1,0:T(8,128)(2,1)S(1)} all-to-all(bf16[32,16,256]{2,1,0:T(8,128)(2,1)S(1)} %add_convert_fusion), channel_id=1, replica_groups=mesh['z'=8,'y'=4,'c'=2,'x'=4] {'z','y'}, dimensions={0} | all-to-all | bytes 524288 | tf_op jit(solution)/shard_map/all_to_all | solution.py:272
  164.5 0.7 copy.41
  (19 shorter events, 0.6 us)
Async XLA Ops:
  3.5 12.2 %copy-start.2 = (s32[64]{0:T(128)S(1)}, s32[64]{0:T(128)}, u32[]{:S(2)}) copy-start(s32[64]{0:T(128)} %order_ref.3) | copy-start | bytes 772
  3.6 14.7 %copy-start.1 = (s32[64,2]{0,1:T(2,128)S(1)}, s32[64,2]{0,1:T(2,128)}, u32[]{:S(2)}) copy-start(s32[64,2]{0,1:T(2,128)} %param.10) | copy-start | bytes 1540
  3.6 86.0 %all-to-all-start = ((bf16[64,1,64,384]{3,2,1,0:T(8,128)(2,1)}), bf16[64,1,64,384]{3,2,1,0:T(8,128)(2,1)S(1)}, u32[]{:S(2)}, u32[]{:S(2)}) async-start(bf16[64,1,64,384]{3,2,1,0:T(8,128)(2,1)} %gather_rows.3), calls=%async_computation | async-start | bytes 6291456 | tf_op jit(solution)/shard_map/all_to_all | solution.py:237
  28.6 6.5 %copy-start.3 = (s32[64]{0:T(128)S(1)}, s32[64]{0:T(128)}, u32[]{:S(2)}) copy-start(s32[64]{0:T(128)} %order_ref.3) | copy-start | bytes 772
  89.6 9.3 %copy-start = (bf16[64,1,64,384]{3,2,1,0:T(8,128)(2,1)}, bf16[64,1,64,384]{3,2,1,0:T(8,128)(2,1)S(1)}, u32[]{:S(2)}) copy-start(bf16[64,1,64,384]{3,2,1,0:T(8,128)(2,1)S(1)} %all-to-all-done) | copy-start | bytes 9437188
  89.6 34.3 %all-to-all-start.1 = ((bf16[64,1,64,128]{3,2,1,0:T(8,128)(2,1)}), bf16[64,1,64,128]{3,2,1,0:T(8,128)(2,1)}, u32[]{:S(2)}, u32[]{:S(2)}) async-start(bf16[64,1,64,128]{3,2,1,0:T(8,128)(2,1)} %gather_rows.2), calls=%async_computation.1 | async-start | bytes 2097152 | tf_op jit(solution)/shard_map/all_to_all | solution.py:254
  133.9 9.3 %all-to-all-start.2 = ((bf16[8,2,16,256]{3,2,1,0:T(8,128)(2,1)}), bf16[8,2,16,256]{3,2,1,0:T(8,128)(2,1)S(1)}, u32[]{:S(2)}, u32[]{:S(2)}) async-start(bf16[8,2,16,256]{3,2,1,0:T(8,128)(2,1)} %contract_last.1), calls=%async_computation.2 | async-start | bytes 262144 | tf_op jit(solution)/shard_map/all_to_all | solution.py:266
where the time goes:
time: 167 us; the launch traced here: 165 us
  Pallas kernels  77.3 us (46%)
  starting transfers between devices  22.7 us (14%)
  waiting for transfers between devices  21.6 us (13%)
  blocking collectives  20.7 us (12%)
  local copies, waits for them, and re-layouts  14.6 us (9%)
  between operations  7.21 us (4%)
    pallas_call x2, Pallas kernels, expand(): pl.pallas_call(functools.partial(expand_kernel, nvec), out_shape=[jax.Sha...  37.8 us
    pallas_call x1, Pallas kernels, contract_first(): pl.pallas_call(first_kernel, out_shape=[sums, sums], grid=(groups // step...  23.2 us
    all_to_all x1, blocking collectives, per_device(): lax.all_to_all(placed.astype(BF16), ('z', 'y'), split_axis=0, concat_axis...  20.7 us
    all_to_all x1, waiting for transfers between devices, per_device(): lax.all_to_all(sent_early, kp, split_axis=0, concat_axis=0, tiled=True)  15.3 us
    all_to_all x1, starting transfers between devices, per_device(): lax.all_to_all(sent_early, kp, split_axis=0, concat_axis=0, tiled=True)  12.1 us
    pallas_call x1, Pallas kernels, contract_last(): pl.pallas_call(functools.partial(last_kernel, step, ahead, pad), out_shap...  10.1 us
    unnamed x11, local copies, waits for them, and re-layouts  6.74 us
    pallas_call x2, Pallas kernels, gather_rows(): pl.pallas_call(functools.partial(gather_kernel, first, width, chunks), ou...  6.25 us
  transfers between devices with their start and end apart: 3, of which 3 were waited for; matrix products, arithmetic and copies ran while one was open for 9% of the time, Pallas kernels for 39%

commit v1 on v0

--- a/solution.py
+++ b/solution.py
@@ -140,24 +140,32 @@
 
 
 def last_kernel(
-    step, ahead, pad, u2_ref, u1_ref, c_hbm, fwd_ref, mir_ref, out_ref, c_ref, u_ref, flip, c_sem, u_sems
+    step, ahead, pad, u2_hbm, u1_hbm, c_hbm, fwd_hbm, mir_hbm, out_hbm,
+    c_ref, u_ref, flip, fwd_ref, mir_ref, fwd_out, mir_out, c_sem, u_sems, sum_sems, out_sems,
 ):
     groups, cols, width = c_ref.shape
     blocks = groups // step
     lanes = step * width
     fetch_c = pltpu.make_async_copy(c_hbm, c_ref, c_sem)
+    fetch_mir = pltpu.make_async_copy(mir_hbm, mir_ref, sum_sems.at[0])
+    fetch_fwd = pltpu.make_async_copy(fwd_hbm, fwd_ref, sum_sems.at[1])
     fetches = [
         pltpu.make_async_copy(
             source.at[:, pl.ds(block * lanes, lanes)],
             u_ref.at[which * blocks + block],
             u_sems.at[which * blocks + block],
         )
-        for which, source in ((0, u1_ref), (1, u2_ref))
+        for which, source in ((0, u1_hbm), (1, u2_hbm))
         for block in range(blocks)
     ]
     fetch_c.start()
-    for index in range(ahead):
+    for index in range(2):
         fetches[index].start()
+    fetch_c.wait()
+    for index in range(2, ahead):
+        fetches[index].start()
+    fetch_mir.start()
+    fetch_fwd.start()
 
     def arrived(index):
         fetches[index].wait()
@@ -165,13 +173,29 @@
             fetches[index + ahead].start()
         return u_ref[index]
 
-    fetch_c.wait()
+    def leave(total, pieces_ref, which):
+        total = total.astype(BF16)
+        pieces, part, half_lanes = pieces_ref.shape
+        parts = cols // part
+        for piece in range(pieces):
+            half, eig = piece // parts, piece % parts
+            pieces_ref[piece] = total[
+                eig * part : (eig + 1) * part, half * half_lanes : (half + 1) * half_lanes
+            ]
+        copy = pltpu.make_async_copy(pieces_ref, out_hbm.at[:, which], out_sems.at[which])
+        copy.start()
+        return copy
+
+    total = jnp.zeros(mir_ref.shape, F32)
+    for block in range(blocks):
+        rows = jnp.concatenate([c_ref[block * step + j] for j in range(step)], axis=1)
+        total = total + product(rows, arrived(block))
+    fetch_mir.wait()
+    mirror_left = leave(total + mir_ref[...], mir_out, 1)
+
     for c in range(groups):
         flip[pl.ds(c * pad, cols)] = c_ref[c].astype(F32)
-    forward, mirror = fwd_ref[...], mir_ref[...]
-    for block in range(blocks):
-        rows = jnp.concatenate([c_ref[block * step + j] for j in range(step)], axis=1)
-        mirror = mirror + product(rows, arrived(block))
+    total = jnp.zeros(fwd_ref.shape, F32)
     for block in range(blocks):
         rows = jnp.concatenate(
             [
@@ -180,16 +204,11 @@
             ],
             axis=1,
         )
-        forward = forward + product(rows, arrived(blocks + block))
-    pieces, _, part, half_lanes = out_ref.shape
-    parts = cols // part
-    for which, total in ((0, forward), (1, mirror)):
-        total = total.astype(BF16)
-        for piece in range(pieces):
-            half, eig = piece // parts, piece % parts
-            out_ref[piece, which] = total[
-                eig * part : (eig + 1) * part, half * half_lanes : (half + 1) * half_lanes
-            ]
+        total = total + product(rows, arrived(blocks + block))
+    fetch_fwd.wait()
+    forward_left = leave(total + fwd_ref[...], fwd_out, 0)
+    mirror_left.wait()
+    forward_left.wait()
 
 
 def contract_last(u2, u1, c, forward, mirror, pieces, step, ahead):
@@ -197,19 +216,25 @@
     groups, cols, width = c.shape
     pad = cols + 8
     copies = 2 * groups // step
-    whole = pl.BlockSpec(memory_space=pltpu.VMEM)
     away = pl.BlockSpec(memory_space=pl.ANY)
+    one_way = (pieces[0],) + pieces[2:]
     return pl.pallas_call(
         functools.partial(last_kernel, step, ahead, pad),
         out_shape=jax.ShapeDtypeStruct(pieces, BF16),
-        in_specs=[away, away, away, whole, whole],
-        out_specs=whole,
+        in_specs=[away] * 5,
+        out_specs=away,
         scratch_shapes=[
             pltpu.VMEM((groups, cols, width), BF16),
             pltpu.VMEM((copies, rows, step * width), BF16),
             pltpu.VMEM((groups * pad, width), F32),
+            pltpu.VMEM(forward.shape, F32),
+            pltpu.VMEM(mirror.shape, F32),
+            pltpu.VMEM(one_way, BF16),
+            pltpu.VMEM(one_way, BF16),
             pltpu.SemaphoreType.DMA,
             pltpu.SemaphoreType.DMA((copies,)),
+            pltpu.SemaphoreType.DMA((2,)),
+            pltpu.SemaphoreType.DMA((2,)),
         ],
         compiler_params=pltpu.CompilerParams(vmem_limit_bytes=60 * MIB),
         cost_estimate=pl.CostEstimate(
@@ -261,7 +286,7 @@
     part_rows = nc_bands // eigs
     half_lanes = nv_bands * nvec // cores
     pieces = (cores * eigs, 2, part_rows, half_lanes)
-    sums = contract_last(u2_late, u1_late, owned_late, forward, mirror, pieces, 8, 4)
+    sums = contract_last(u2_late, u1_late, owned_late, forward, mirror, pieces, 8, 6)
 
     arrived = lax.all_to_all(sums, ("c", "x"), split_axis=0, concat_axis=0, tiled=True)
     arrived = arrived.reshape(cores, eigs, 2, part_rows, half_lanes).astype(F32).sum(1)

time: 167 us -> 166 us (level)
  no operation moved by 1% of the time
where the time goes in v1:
time: 166 us; the launch traced here: 164 us
  Pallas kernels  76.3 us (46%)
  starting transfers between devices  22.7 us (14%)
  waiting for transfers between devices  21.6 us (13%)
  blocking collectives  20.7 us (12%)
  local copies, waits for them, and re-layouts  14.6 us (9%)
  between operations  7.21 us (4%)
    pallas_call x2, Pallas kernels, expand(): pl.pallas_call(functools.partial(expand_kernel, nvec), out_shape=[jax.Sha...  37.8 us
    pallas_call x1, Pallas kernels, contract_first(): pl.pallas_call(first_kernel, out_shape=[sums, sums], grid=(groups // step...  23.2 us
    all_to_all x1, blocking collectives, per_device(): lax.all_to_all(placed.astype(BF16), ('z', 'y'), split_axis=0, concat_axis...  20.7 us
    all_to_all x1, waiting for transfers between devices, per_device(): lax.all_to_all(sent_early, kp, split_axis=0, concat_axis=0, tiled=True)  15.3 us
    all_to_all x1, starting transfers between devices, per_device(): lax.all_to_all(sent_early, kp, split_axis=0, concat_axis=0, tiled=True)  12.1 us
    pallas_call x1, Pallas kernels, contract_last(): pl.pallas_call(functools.partial(last_kernel, step, ahead, pad), out_shap...  9.11 us
    unnamed x11, local copies, waits for them, and re-layouts  6.74 us
    pallas_call x2, Pallas kernels, gather_rows(): pl.pallas_call(functools.partial(gather_kernel, first, width, chunks), ou...  6.25 us
  transfers between devices with their start and end apart: 3, of which 3 were waited for; matrix products, arithmetic and copies ran while one was open for 9% of the time, Pallas kernels for 39%

profile of v1, /device:TPU:2, one launch (start us, length us, event | category | flops | bytes accessed | tf_op | source)
XLA Modules:
  0.0 164.2 jit_solution(10838357051016438978)
XLA Ops:
  0.0 3.5 %gather_rows.3 = bf16[64,1,64,384]{3,2,1,0:T(8,128)(2,1)} custom-call(s32[64]{0:T(128)} %order_ref.3, bf16[64,1,64,512]{3,2,1,0:T(8,128)(2,1)} %cond_ref.3), custom_call_target="tpu_custom_call" | custom-call | bytes 6291456 | tf_op jit(solution)/shard_map/gather_rows/pallas_call | solution.py:39
  3.6 12.1 %all-to-all-start = ((bf16[64,1,64,384]{3,2,1,0:T(8,128)(2,1)}), bf16[64,1,64,384]{3,2,1,0:T(8,128)(2,1)S(1)}, u32[]{:S(2)}, u32[]{:S(2)}) async-start(bf16[64,1,64,384]{3,2,1,0:T(8,128)(2,1)} %gather_rows.3), calls=%async_computation | async-start | bytes 6291456 | tf_op jit(solution)/shard_map/all_to_all | solution.py:262
  15.7 0.6 dynamic_slice.15
  18.3 0.5 fusion
  22.8 2.7 %gather_rows.2 = bf16[64,1,64,128]{3,2,1,0:T(8,128)(2,1)} custom-call(s32[64]{0:T(128)} %order_ref.3, bf16[64,1,64,512]{3,2,1,0:T(8,128)(2,1)} %cond_ref.3), custom_call_target="tpu_custom_call" | custom-call | bytes 2097152 | tf_op jit(solution)/shard_map/gather_rows/pallas_call | solution.py:39
  26.8 0.9 constant_dynamic-slice_fusion
  27.7 0.1 copy.43
  27.8 0.8 copy.33
  28.6 6.5 %copy.45 = bf16[1,64,64,512]{3,1,2,0:T(8,128)(2,1)} copy(bf16[1,64,64,512]{3,2,1,0:T(8,128)(2,1)} %param.7) | data formatting | bytes 8388608 | tf_op args[1]
  35.2 0.6 gather_fusion
  35.7 0.7 multiply_bitcast_fusion.x_ref
  36.4 18.9 %expand.3 = (bf16[512,24576]{1,0:T(8,128)(2,1)}, bf16[512,8192]{1,0:T(8,128)(2,1)}) custom-call(bf16[512,64]{1,0:T(8,128)(2,1)} %multiply_bitcast_fusion.x_ref, bf16[64,64,512]{2,1,0:T(8,128)(2,1)} %bitcast.47, f32[1,512]{1,0:T(1,128)} %bitcast.51), custom_call_target="tpu_custom_call" | custom-call | flops 2147483648 | bytes 37748736 | tf_op jit(solution)/shard_map/expand/pallas_call | solution.py:80
  55.3 18.9 %expand.2 = (bf16[512,24576]{1,0:T(8,128)(2,1)}, bf16[512,8192]{1,0:T(8,128)(2,1)}) custom-call(bf16[512,64]{1,0:T(8,128)(2,1)} %bitcast.50, bf16[64,64,512]{2,1,0:T(8,128)(2,1)} %bitcast.46, f32[1,512]{1,0:T(1,128)} %bitcast.52), custom_call_target="tpu_custom_call" | custom-call | flops 2147483648 | bytes 37748736 | tf_op jit(solution)/shard_map/expand/pallas_call | solution.py:80
  74.3 15.3 %all-to-all-done = bf16[64,1,64,384]{3,2,1,0:T(8,128)(2,1)S(1)} async-done(((bf16[64,1,64,384]{3,2,1,0:T(8,128)(2,1)}), bf16[64,1,64,384]{3,2,1,0:T(8,128)(2,1)S(1)}, u32[]{:S(2)}, u32[]{:S(2)}) %all-to-all-start) | async-done | bytes 3145760 | tf_op jit(solution)/shard_map/all_to_all | solution.py:262
  89.6 5.7 %all-to-all-start.1 = ((bf16[64,1,64,128]{3,2,1,0:T(8,128)(2,1)}), bf16[64,1,64,128]{3,2,1,0:T(8,128)(2,1)}, u32[]{:S(2)}, u32[]{:S(2)}) async-start(bf16[64,1,64,128]{3,2,1,0:T(8,128)(2,1)} %gather_rows.2), calls=%async_computation.1 | async-start | bytes 2097152 | tf_op jit(solution)/shard_map/all_to_all | solution.py:279
  95.3 3.6 %copy.38.ct_ref = bf16[64,64,384]{2,1,0:T(8,128)(2,1)} copy(bf16[64,64,384]{2,0,1:T(8,128)(2,1)S(1)} %bitcast.44) | data formatting | bytes 6291456 | tf_op jit(solution)/shard_map/transpose | solution.py:284
  98.9 23.2 %contract_first.1 = (f32[64,512]{1,0:T(8,128)}, f32[64,512]{1,0:T(8,128)}) custom-call(bf16[512,24576]{1,0:T(8,128)(2,1)} %get-tuple-element.22.u2_ref, bf16[64,64,384]{2,1,0:T(8,128)(2,1)} %copy.38.ct_ref, bf16[512,24576]{1,0:T(8,128)(2,1)} %get-tuple-element.24.u1_ref, bf16[64,64,384]{2,1,0:T(8,128)(2,1)} %bitcast.45), custom_call_target="tpu_custom_call" | custom-call | flops 3221225472 | bytes 56623104 | tf_op jit(solution)/shard_map/contract_first/pallas_call | solution.py:126
  122.1 1.8 %all-to-all-done.1 = bf16[64,1,64,128]{3,2,1,0:T(8,128)(2,1)} async-done(((bf16[64,1,64,128]{3,2,1,0:T(8,128)(2,1)}), bf16[64,1,64,128]{3,2,1,0:T(8,128)(2,1)}, u32[]{:S(2)}, u32[]{:S(2)}) %all-to-all-start.1) | async-done | bytes 1048608 | tf_op jit(solution)/shard_map/all_to_all | solution.py:279
  123.9 9.1 %contract_last.1 = bf16[8,2,16,256]{3,2,1,0:T(8,128)(2,1)} custom-call(bf16[512,8192]{1,0:T(8,128)(2,1)} %get-tuple-element.19.u2_hbm, bf16[512,8192]{1,0:T(8,128)(2,1)} %get-tuple-element.20.u1_hbm, bf16[64,64,128]{2,1,0:T(8,128)(2,1)} %bitcast.12.c_hbm, f32[64,512]{1,0:T(8,128)} %get-tuple-element.25.fwd_hbm, f32[64,512]{1,0:T(8,128)} %get-tuple-element.26.mir_hbm), custom_call_target="tpu_custom_call" | custom-call | flops 1073741824 | bytes 18874368 | tf_op jit(solution)/shard_map/contract_last/pallas_call | solution.py:221
  133.0 4.8 %all-to-all-start.2 = ((bf16[8,2,16,256]{3,2,1,0:T(8,128)(2,1)}), bf16[8,2,16,256]{3,2,1,0:T(8,128)(2,1)S(1)}, u32[]{:S(2)}, u32[]{:S(2)}) async-start(bf16[8,2,16,256]{3,2,1,0:T(8,128)(2,1)} %contract_last.1), calls=%async_computation.2 | async-start | bytes 262144 | tf_op jit(solution)/shard_map/all_to_all | solution.py:291
  137.8 4.5 %all-to-all-done.2 = bf16[8,2,16,256]{3,2,1,0:T(8,128)(2,1)S(1)} async-done(((bf16[8,2,16,256]{3,2,1,0:T(8,128)(2,1)}), bf16[8,2,16,256]{3,2,1,0:T(8,128)(2,1)S(1)}, u32[]{:S(2)}, u32[]{:S(2)}) %all-to-all-start.2) | async-done | bytes 131104 | tf_op jit(solution)/shard_map/all_to_all | solution.py:291
  142.4 0.2 add_convert_fusion
  142.6 20.7 %all_to_all.20 = bf16[32,16,256]{2,1,0:T(8,128)(2,1)S(1)} all-to-all(bf16[32,16,256]{2,1,0:T(8,128)(2,1)S(1)} %add_convert_fusion), channel_id=1, replica_groups=mesh['z'=8,'y'=4,'c'=2,'x'=4] {'z','y'}, dimensions={0} | all-to-all | bytes 524288 | tf_op jit(solution)/shard_map/all_to_all | solution.py:297
  163.5 0.7 copy.41
  (19 shorter events, 0.6 us)
Async XLA Ops:
  3.5 12.2 %copy-start.2 = (s32[64]{0:T(128)S(1)}, s32[64]{0:T(128)}, u32[]{:S(2)}) copy-start(s32[64]{0:T(128)} %order_ref.3) | copy-start | bytes 772
  3.6 14.7 %copy-start.1 = (s32[64,2]{0,1:T(2,128)S(1)}, s32[64,2]{0,1:T(2,128)}, u32[]{:S(2)}) copy-start(s32[64,2]{0,1:T(2,128)} %param.10) | copy-start | bytes 1540
  3.6 86.0 %all-to-all-start = ((bf16[64,1,64,384]{3,2,1,0:T(8,128)(2,1)}), bf16[64,1,64,384]{3,2,1,0:T(8,128)(2,1)S(1)}, u32[]{:S(2)}, u32[]{:S(2)}) async-start(bf16[64,1,64,384]{3,2,1,0:T(8,128)(2,1)} %gather_rows.3), calls=%async_computation | async-start | bytes 6291456 | tf_op jit(solution)/shard_map/all_to_all | solution.py:262
  28.6 6.5 %copy-start.3 = (s32[64]{0:T(128)S(1)}, s32[64]{0:T(128)}, u32[]{:S(2)}) copy-start(s32[64]{0:T(128)} %order_ref.3) | copy-start | bytes 772
  89.6 9.3 %copy-start = (bf16[64,1,64,384]{3,2,1,0:T(8,128)(2,1)}, bf16[64,1,64,384]{3,2,1,0:T(8,128)(2,1)S(1)}, u32[]{:S(2)}) copy-start(bf16[64,1,64,384]{3,2,1,0:T(8,128)(2,1)S(1)} %all-to-all-done) | copy-start | bytes 9437188
  89.6 34.3 %all-to-all-start.1 = ((bf16[64,1,64,128]{3,2,1,0:T(8,128)(2,1)}), bf16[64,1,64,128]{3,2,1,0:T(8,128)(2,1)}, u32[]{:S(2)}, u32[]{:S(2)}) async-start(bf16[64,1,64,128]{3,2,1,0:T(8,128)(2,1)} %gather_rows.2), calls=%async_computation.1 | async-start | bytes 2097152 | tf_op jit(solution)/shard_map/all_to_all | solution.py:279
  133.0 9.3 %all-to-all-start.2 = ((bf16[8,2,16,256]{3,2,1,0:T(8,128)(2,1)}), bf16[8,2,16,256]{3,2,1,0:T(8,128)(2,1)S(1)}, u32[]{:S(2)}, u32[]{:S(2)}) async-start(bf16[8,2,16,256]{3,2,1,0:T(8,128)(2,1)} %contract_last.1), calls=%async_computation.2 | async-start | bytes 262144 | tf_op jit(solution)/shard_map/all_to_all | solution.py:291
